TPU v7x, 32 devices: a whole 2x2x4 slice. The times are simulated.
32 devices in a mesh: row: 8 (over y, x, core), col: 4 (over z).
Axes of the slice: x: 2, y: 2, z: 4, core: 2. Of those that a mesh axis runs over, the one named last changes fastest.
Arguments:
- inputs: bfloat16 [512, 16384], P('col', 'row'), may hold values from -6 to 6
- gate_weight: bfloat16 [16384, 26624], P('row', 'col'), may hold values from -0.0625 to 0.0625
- up_weight: bfloat16 [16384, 26624], P('row', 'col'), may hold values from -0.0625 to 0.0625
- gate_pattern: int32 [128, 208], P('row', 'col'), may hold values 0 or 1
- up_pattern: int32 [128, 208], P('row', 'col'), may hold values 0 or 1
- cotangent: bfloat16 [512, 26624], P('row', 'col'), may hold values from -6 to 6
Outputs:
- hidden: bfloat16 [512, 26624], P('row', 'col')
- input_grad: bfloat16 [512, 16384], P('col', 'row')
All inputs are finite; a program needn't handle non-finite values. No bound on the sum of `gate_pattern` or of `up_pattern` on one device may be relied on, other than what follows from the above.
Results may differ from a plain program's by a relative error of at most 0.039.
Values may be sent and summed in bfloat16 or wider, within the bound.
No kernel may reach another device: no remote copies, remote signals or barrier semaphores. Data moves between devices by JAX's collectives and lax.ppermute only.
A program may use at most 256 MiB of HBM per device.

v0:
```python
import jax
import jax.numpy as jnp
from jax import lax
from jax.sharding import PartitionSpec as P

BLOCK = 128


def expand(weight, pattern):
    height, breadth = weight.shape
    flags = pattern.astype(weight.dtype)
    tiles = (
        weight.reshape(height // BLOCK, BLOCK, breadth // BLOCK, BLOCK) * flags[:, None, :, None]
    )
    return tiles.reshape(height, breadth)


def derivatives(summed, cotangent, local_hidden):
    gate_sum = summed[:, :local_hidden]
    up_sum = summed[:, local_hidden:]
    sigmoid_gate = jax.nn.sigmoid(gate_sum)
    activated = gate_sum * sigmoid_gate
    hidden = (activated * up_sum).astype(jnp.bfloat16)
    cotangent_f = cotangent.astype(jnp.float32)
    gate_grad = (
        cotangent_f * up_sum * sigmoid_gate * (1.0 + gate_sum * (1.0 - sigmoid_gate))
    ).astype(jnp.bfloat16)
    up_grad = (cotangent_f * activated).astype(jnp.bfloat16)
    return (hidden, jnp.concatenate([gate_grad, up_grad], axis=1))


def shards(inputs, gate_weight, up_weight, gate_pattern, up_pattern, cotangent):
    local_hidden = gate_weight.shape[1]
    stacked_weights = jnp.concatenate(
        [expand(gate_weight, gate_pattern), expand(up_weight, up_pattern)], axis=1
    )
    partial_sums = jnp.dot(
        lax.all_gather(inputs, "col", axis=0, tiled=True),
        stacked_weights,
        preferred_element_type=jnp.float32,
    )
    summed = lax.psum_scatter(
        partial_sums.astype(jnp.bfloat16), "row", scatter_dimension=0, tiled=True
    ).astype(jnp.float32)
    hidden, gradients = derivatives(summed, cotangent, local_hidden)
    gradient_term = lax.dot_general(
        lax.all_gather(gradients, "row", axis=0, tiled=True),
        stacked_weights,
        (((1,), (1,)), ((), ())),
        preferred_element_type=jnp.float32,
    )
    input_grad = lax.psum_scatter(
        gradient_term.astype(jnp.bfloat16), "col", scatter_dimension=0, tiled=True
    )
    return (hidden, input_grad)


def solution(mesh):
    placed = (
        P("col", "row"),
        P("row", "col"),
        P("row", "col"),
        P("row", "col"),
        P("row", "col"),
        P("row", "col"),
    )
    return jax.shard_map(
        shards,
        mesh=mesh,
        in_specs=placed,
        out_specs=(P("row", "col"), P("col", "row")),
        check_vma=False,
    )
```

profile of v0, /device:TPU:0, one launch (start us, length us, event | category | flops | bytes accessed | tf_op | source)
XLA Modules:
  0.0 498.5 jit_solution(14436189573204188208)
XLA Ops:
  7.2 0.0 all-gather.3.cloned.1.call-start
  7.2 0.7 all-gather.3.cloned.1.call-update
  7.9 0.0 reduce-scatter.7.cloned.1.call-start
  7.9 0.7 convert_element_type.30
  8.6 0.1 copy.16
  8.8 0.7 convert_element_type.31
  9.5 0.1 copy.18
  9.6 36.4 %copy.17 = bf16[2048,6656]{0,1:T(8,128)(2,1)} copy(bf16[2048,6656]{1,0:T(8,128)(2,1)} %param.7) | data formatting | bytes 54525952 | tf_op args[1]
  46.0 34.3 %copy.19 = bf16[2048,6656]{0,1:T(8,128)(2,1)} copy(bf16[2048,6656]{1,0:T(8,128)(2,1)} %param.8) | data formatting | bytes 54525952 | tf_op args[2]
  80.3 9.4 %mul.43 = bf16[16,128,52,128]{1,0,3,2:T(8,128)(2,1)} broadcast(bf16[16,52]{0,1:T(8,128)(2,1)S(1)} %copy.16), dimensions={0,2} | broadcast | bytes 27264640 | tf_op jit(solution)/shard_map/mul | solution.py:13
  89.7 9.3 %mul.46 = bf16[16,128,52,128]{1,0,3,2:T(8,128)(2,1)} broadcast(bf16[16,52]{0,1:T(8,128)(2,1)S(1)} %copy.18), dimensions={0,2} | broadcast | bytes 27264640 | tf_op jit(solution)/shard_map/mul | solution.py:13
  99.0 56.6 %bitcast_multiply_fusion = (bf16[2048,6656]{0,1:T(8,128)(2,1)}, bf16[2048,6656]{0,1:T(8,128)(2,1)}) fusion(bf16[2048,6656]{0,1:T(8,128)(2,1)} %copy.19, bf16[832,8,16,128]{3,2,1,0:T(8,128)(2,1)} %bitcast.18, bf16[2048,6656]{0,1:T(8,128)(2,1)} %copy.17, bf16[832,8,16,128]{3,2,1,0:T(8,128)(2,1)} %bitcast.17), kind=kLoop, calls=%fused_computation.3 | loop fusion | flops 27262976 | bytes 163577856 | tf_op jit(solution)/shard_map/mul | solution.py:13
  155.6 37.4 %fusion.3 = bf16[512,13312]{0,1:T(8,128)(2,1)} fusion(bf16[512,2048]{1,0:T(8,128)(2,1)} %all-gather.3.cloned.1.call-done, bf16[2048,6656]{0,1:T(8,128)(2,1)} %get-tuple-element.11, bf16[2048,6656]{0,1:T(8,128)(2,1)} %get-tuple-element.12), kind=kOutput, calls=%fused_computation.6 | convolution fusion | flops 28033155072 | bytes 70254592 | tf_op jit(solution)/shard_map/dot_general | solution.py:37
  193.0 17.5 %copy.23 = bf16[512,13312]{1,0:T(8,128)(2,1)} copy(bf16[512,13312]{0,1:T(8,128)(2,1)} %fusion.3) | data formatting | bytes 27262976
  210.5 0.0 reduce-scatter.7.cloned.1.call-update
  210.5 0.2 all-gather.5.cloned.1.call-start
  210.7 0.9 copy-done.1
  211.6 1.6 copy.20
  213.2 98.1 %reduce-scatter.7.cloned.1.call-done = bf16[64,13312]{1,0:T(8,128)(2,1)} async-done(((bf16[512,13312]{1,0:T(8,128)(2,1)}), bf16[64,13312]{1,0:T(8,128)(2,1)}) %reduce-scatter.7.cloned.1.call-update) | async-done | bytes 1703952
  311.4 3.3 copy.24
  314.7 0.5 convert_element_type.34
  315.2 4.2 fusion.6
  319.4 11.9 %pad_maximum_fusion.7 = bf16[64,13312]{0,1:T(8,128)(2,1)S(1)} fusion(bf16[64,6656]{0,1:T(8,128)(2,1)S(1)} %get-tuple-element.9, bf16[64,6656]{0,1:T(8,128)(2,1)S(1)} %get-tuple-element.8), kind=kLoop, calls=%fused_computation.13 | loop fusion | flops 3407872 | bytes 3407872 | tf_op jit(solution)/shard_map/concatenate | solution.py:29
  331.3 2.6 copy.21
  333.9 0.0 all-gather.5.cloned.1.call-update
  334.0 0.3 reduce-scatter.5.cloned.1.call-start
  334.2 76.4 %all-gather.5.cloned.1.call-done = bf16[512,13312]{1,0:T(8,128)(2,1)} async-done(((bf16[64,13312]{1,0:T(8,128)(2,1)}), bf16[512,13312]{1,0:T(8,128)(2,1)}) %all-gather.5.cloned.1.call-update) | async-done | bytes 13631504 | tf_op jit(solution)/shard_map/all_gather | solution.py:47
  410.6 37.3 %fusion.9 = bf16[512,2048]{1,0:T(8,128)(2,1)} fusion(bf16[512,13312]{1,0:T(8,128)(2,1)} %all-gather.5.cloned.1.call-done, bf16[2048,6656]{0,1:T(8,128)(2,1)} %get-tuple-element.11, bf16[2048,6656]{0,1:T(8,128)(2,1)} %get-tuple-element.12), kind=kOutput, calls=%fused_computation.17 | convolution fusion | flops 28027387904 | bytes 70254592 | tf_op jit(solution)/shard_map/dot_general | solution.py:46
  447.9 0.0 reduce-scatter.5.cloned.1.call-update
  447.9 0.0 copy-done
  447.9 1.5 copy.22
  449.4 42.5 %reduce-scatter.5.cloned.1.call-done = bf16[128,2048]{1,0:T(8,128)(2,1)} async-done(((bf16[512,2048]{1,0:T(8,128)(2,1)}), bf16[128,2048]{1,0:T(8,128)(2,1)}) %reduce-scatter.5.cloned.1.call-update) | async-done | bytes 524304 | tf_op jit(solution)/shard_map/reduce_scatter | solution.py:52
  (3 shorter events, 0.0 us)
Async XLA Ops:
  7.2 148.4 %all-gather.3.cloned.1.call-start = ((), (), s32[]{:S(2)}) async-start(), calls=%async_computation.2 | async-start | bytes 2621440 | tf_op jit(solution)/shard_map/all_gather | solution.py:38
  7.9 303.5 %reduce-scatter.7.cloned.1.call-start = ((), (), s32[]{:S(2)}) async-start(), calls=%async_computation.5 | async-start | bytes 15335424
  210.5 1.2 copy-start.1
  210.5 200.2 %all-gather.5.cloned.1.call-start = ((), (), s32[]{:S(2)}) async-start(), calls=%async_computation.3 | async-start | bytes 15335424 | tf_op jit(solution)/shard_map/all_gather | solution.py:47
  334.0 114.0 %copy-start = (bf16[64,6656]{0,1:T(8,128)(2,1)S(1)}, bf16[64,6656]{0,1:T(8,128)(2,1)}, u32[]{:S(2)}) copy-start(bf16[64,6656]{0,1:T(8,128)(2,1)} %get-tuple-element.10) | copy-start | bytes 2555908
  334.0 158.0 %reduce-scatter.5.cloned.1.call-start = ((), (), s32[]{:S(2)}) async-start(), calls=%async_computation.4 | async-start | bytes 2621440 | tf_op jit(solution)/shard_map/reduce_scatter | solution.py:52
Sparse Core Ops, SparseCore 0:
  9.6 48.6 all-gather.2
  210.6 100.7 reduce-scatter.6
  334.1 76.5 all-gather.4
  448.0 43.8 reduce-scatter.4
where the time goes:
time: 501 us; the launch traced here: 498 us
  waiting for transfers between devices  218 us (44%)
  local copies, waits for them, and re-layouts  117 us (23%)
  matrix products  74.7 us (15%)
  other arithmetic  74.5 us (15%)
  between operations  13.8 us (3%)
    unnamed x5, waiting for transfers between devices  98.9 us
    unnamed x10, local copies, waits for them, and re-layouts  95.6 us
    all_gather x1, waiting for transfers between devices, shards(): lax.all_gather(gradients, 'row', axis=0, tiled=True)  76.4 us
    mul x1, other arithmetic, expand(): weight.reshape(height // BLOCK, BLOCK, breadth // BLOCK, BLOCK)  56.6 us
    reduce_scatter x1, waiting for transfers between devices, shards(): lax.psum_scatter(gradient_term.astype(jnp.bfloat16), 'col', scatter_dimen...  42.5 us
    dot_general x1, matrix products, shards(): jnp.dot(lax.all_gather(inputs, 'col', axis=0, tiled=True), stacked_weight...  37.4 us
    dot_general x1, matrix products, shards(): lax.dot_general(lax.all_gather(gradients, 'row', axis=0, tiled=True), sta...  37.3 us
    mul x2, local copies, waits for them, and re-layouts, expand(): weight.reshape(height // BLOCK, BLOCK, breadth // BLOCK, BLOCK)  18.7 us
  transfers between devices with their start and end apart: 4, of which 3 were waited for; matrix products, arithmetic and copies ran while one was open for 30% of the time, Pallas kernels for 0%

commit v1 on v0

v1 whole, which is shorter than its diff:
```python
import functools

import jax
import jax.numpy as jnp
from jax import lax
from jax.experimental import pallas as pl
from jax.experimental.pallas import tpu as pltpu
from jax.sharding import PartitionSpec as P

BLOCK = 128
TOKEN_CHUNKS = 2
HIDDEN_CHUNKS = 2
VMEM_BYTES = 48 * 1024 * 1024


def masked(w_ref, f_ref):
    return jnp.concatenate(
        [
            w_ref[k * BLOCK : (k + 1) * BLOCK, :] * f_ref[k : k + 1, :]
            for k in range(w_ref.shape[0] // BLOCK)
        ],
        axis=0,
    )


def forward_kernel(x_ref, wg_ref, wu_ref, fg_ref, fu_ref, og_ref, ou_ref):
    for w_ref, f_ref, o_ref in ((wg_ref, fg_ref, og_ref), (wu_ref, fu_ref, ou_ref)):
        o_ref[...] = jnp.dot(
            x_ref[...], masked(w_ref, f_ref), preferred_element_type=jnp.float32
        ).astype(jnp.bfloat16)


def forward(x, weights, flags, first, tiles, tile):
    rows, depth = x.shape
    blocks = flags[0].shape[0]
    w_spec = pl.BlockSpec((depth, tile), lambda i: (0, first + i))
    f_spec = pl.BlockSpec((blocks, tile), lambda i: (0, first + i))
    o_spec = pl.BlockSpec((rows, tile), lambda i: (0, i))
    out = jax.ShapeDtypeStruct((rows, tiles * tile), jnp.bfloat16)
    return pl.pallas_call(
        forward_kernel,
        grid=(tiles,),
        in_specs=[pl.BlockSpec((rows, depth), lambda i: (0, 0)), w_spec, w_spec, f_spec, f_spec],
        out_specs=[o_spec, o_spec],
        out_shape=[out, out],
        compiler_params=pltpu.CompilerParams(vmem_limit_bytes=VMEM_BYTES),
        cost_estimate=pl.CostEstimate(
            flops=4 * rows * depth * tiles * tile,
            bytes_accessed=4 * tiles * tile * (depth + rows) + 2 * rows * depth,
            transcendentals=0,
        ),
    )(x, *weights, *flags)


def backward_kernel(steps, last, a_ref, gg_ref, gu_ref, wg_ref, wu_ref, fg_ref, fu_ref, o_ref, acc):
    i = pl.program_id(0)
    contract = (((1,), (1,)), ((), ()))

    @pl.when(i == 0)
    def _():
        if a_ref is None:
            acc[...] = jnp.zeros_like(acc)
        else:
            acc[...] = a_ref[...]

    for g_ref, w_ref, f_ref in ((gg_ref, wg_ref, fg_ref), (gu_ref, wu_ref, fu_ref)):
        acc[...] += lax.dot_general(
            g_ref[...], masked(w_ref, f_ref), contract, preferred_element_type=jnp.float32
        )

    @pl.when(i == steps - 1)
    def _():
        o_ref[...] = acc[...].astype(o_ref.dtype)


def backward(carry, grads, weights, flags, first, tiles, tile, last):
    rows = grads[0].shape[0]
    blocks, _ = flags[0].shape
    depth = weights[0].shape[0]
    whole = pl.BlockSpec((rows, depth), lambda i: (0, 0))
    w_spec = pl.BlockSpec((depth, tile), lambda i: (0, first + i))
    f_spec = pl.BlockSpec((blocks, tile), lambda i: (0, first + i))
    g_spec = pl.BlockSpec((rows, tile), lambda i: (0, i))
    kernel = functools.partial(backward_kernel, tiles, last)
    if carry is None:
        kernel = functools.partial(backward_kernel, tiles, last, None)
    return pl.pallas_call(
        kernel,
        grid=(tiles,),
        in_specs=([] if carry is None else [whole])
        + [g_spec, g_spec, w_spec, w_spec, f_spec, f_spec],
        out_specs=whole,
        out_shape=jax.ShapeDtypeStruct((rows, depth), jnp.bfloat16 if last else jnp.float32),
        scratch_shapes=[pltpu.VMEM((rows, depth), jnp.float32)],
        compiler_params=pltpu.CompilerParams(vmem_limit_bytes=VMEM_BYTES),
        cost_estimate=pl.CostEstimate(
            flops=4 * rows * depth * tiles * tile,
            bytes_accessed=4 * tiles * tile * (depth + rows) + 2 * rows * depth,
            transcendentals=0,
        ),
    )(*(() if carry is None else (carry,)), *grads, *weights, *flags)


def derivatives(gate_sum, up_sum, cotangent):
    gate_sum = gate_sum.astype(jnp.float32)
    up_sum = up_sum.astype(jnp.float32)
    sigmoid_gate = jax.nn.sigmoid(gate_sum)
    activated = gate_sum * sigmoid_gate
    hidden = (activated * up_sum).astype(jnp.bfloat16)
    cotangent_f = cotangent.astype(jnp.float32)
    gate_grad = (
        cotangent_f * up_sum * sigmoid_gate * (1.0 + gate_sum * (1.0 - sigmoid_gate))
    ).astype(jnp.bfloat16)
    up_grad = (cotangent_f * activated).astype(jnp.bfloat16)
    return hidden, gate_grad, up_grad


def shards(inputs, gate_weight, up_weight, gate_pattern, up_pattern, cotangent):
    depth, local_hidden = gate_weight.shape
    share = cotangent.shape[0]
    piece = share // TOKEN_CHUNKS
    tile = 512 if local_hidden % 512 == 0 else 256
    n_tiles = local_hidden // tile
    bounds = [n_tiles * c // HIDDEN_CHUNKS for c in range(HIDDEN_CHUNKS + 1)]
    weights = (gate_weight, up_weight)
    flags = tuple(
        jnp.repeat(p.astype(jnp.bfloat16), BLOCK, axis=1) for p in (gate_pattern, up_pattern)
    )

    by_chunk = inputs.reshape(-1, TOKEN_CHUNKS, piece, depth)
    xs = [
        lax.all_gather(by_chunk[:, t].reshape(-1, depth), "col", axis=0, tiled=True)
        for t in range(TOKEN_CHUNKS)
    ]
    sums = {}
    for t in range(TOKEN_CHUNKS):
        for c in range(HIDDEN_CHUNKS):
            parts = forward(
                xs[t], weights, flags, bounds[c], bounds[c + 1] - bounds[c], tile
            )
            sums[t, c] = [
                lax.psum_scatter(p, "row", scatter_dimension=0, tiled=True) for p in parts
            ]
    hidden, input_grad = [], []
    for t in range(TOKEN_CHUNKS):
        rows = slice(t * piece, (t + 1) * piece)
        hidden_row = []
        carry = None
        for c in range(HIDDEN_CHUNKS):
            columns = slice(bounds[c] * tile, bounds[c + 1] * tile)
            h, gate_grad, up_grad = derivatives(*sums[t, c], cotangent[rows, columns])
            hidden_row.append(h)
            grads = [
                lax.all_gather(g, "row", axis=0, tiled=True) for g in (gate_grad, up_grad)
            ]
            carry = backward(
                carry,
                grads,
                weights,
                flags,
                bounds[c],
                bounds[c + 1] - bounds[c],
                tile,
                c == HIDDEN_CHUNKS - 1,
            )
        hidden.append(jnp.concatenate(hidden_row, axis=1))
        summed = lax.psum_scatter(carry, "col", scatter_dimension=0, tiled=True)
        input_grad.append(summed.reshape(-1, 1, piece, depth))
    return (
        jnp.concatenate(hidden, axis=0),
        jnp.concatenate(input_grad, axis=1).reshape(-1, depth),
    )


def solution(mesh):
    placed = (
        P("col", "row"),
        P("row", "col"),
        P("row", "col"),
        P("row", "col"),
        P("row", "col"),
        P("row", "col"),
    )
    return jax.shard_map(
        shards,
        mesh=mesh,
        in_specs=placed,
        out_specs=(P("row", "col"), P("col", "row")),
        check_vma=False,
    )
```

time: 501 us -> 701 us (1.40)
  waiting for transfers between devices: 218 us -> 538 us
  Pallas kernels: 0 us -> 117 us
  local copies, waits for them, and re-layouts: 117 us -> 20.8 us
  matrix products: 74.7 us -> 0 us
  other arithmetic: 74.5 us -> 8.61 us
    reduce_scatter x1 -> x10, waiting for transfers between devices: 42.5 us -> 323 us  [the longest x8 286 us: shards(): lax.psum_scatter(p, 'row', scatter_dimension=0, tiled=True)]
    all_gather x2 -> x10, waiting for transfers between devices: 76.4 us -> 210 us  [the longest x8 166 us: shards(): lax.all_gather(g, 'row', axis=0, tiled=True)]
    pallas_call x0 -> x8, Pallas kernels: none -> 117 us  [the longest x4 58.9 us: backward(): pl.pallas_call(kernel, grid=(tiles,), in_specs=([] if carry is None else...]
    unnamed x5 -> x20, waiting for transfers between devices: 98.9 us -> 6.28 us
    unnamed x10 -> x30, local copies, waits for them, and re-layouts: 95.6 us -> 17.7 us
    dot_general x2 -> x0, matrix products: 74.7 us -> none  [the longest x1 37.4 us: shards(): jnp.dot(lax.all_gather(inputs, 'col', axis=0, tiled=True), stacked_weight...]
    mul x1 -> x0, other arithmetic: 56.6 us -> none  [expand(): weight.reshape(height // BLOCK, BLOCK, breadth // BLOCK, BLOCK)]
    mul x2 -> x0, local copies, waits for them, and re-layouts: 18.7 us -> none  [expand(): weight.reshape(height // BLOCK, BLOCK, breadth // BLOCK, BLOCK)]
  transfers between devices with their start and end apart: 4 -> 20, of which waited for: 3 -> 19; matrix products, arithmetic and copies ran while one was open for 30% -> 1% of each run, Pallas kernels for 0% -> 17%
where the time goes in v1:
time: 701 us
  waiting for transfers between devices  538 us (77%)
  Pallas kernels  117 us (17%)
  local copies, waits for them, and re-layouts  20.8 us (3%)
  between operations  14.4 us (2%)
  other arithmetic  8.61 us (1%)
    reduce_scatter x8, waiting for transfers between devices, shards(): lax.psum_scatter(p, 'row', scatter_dimension=0, tiled=True)  286 us
    all_gather x8, waiting for transfers between devices, shards(): lax.all_gather(g, 'row', axis=0, tiled=True)  166 us
    pallas_call x4, Pallas kernels, backward(): pl.pallas_call(kernel, grid=(tiles,), in_specs=([] if carry is None else...  58.9 us
    pallas_call x4, Pallas kernels, forward(): pl.pallas_call(forward_kernel, grid=(tiles,), in_specs=[pl.BlockSpec((row...  58.4 us
    all_gather x2, waiting for transfers between devices, shards(): lax.all_gather(by_chunk[:, t].reshape(-1, depth), 'col', axis=0, tiled=True)  43.5 us
    reduce_scatter x2, waiting for transfers between devices, shards(): summed = lax.psum_scatter(carry, 'col', scatter_dimension=0, tiled=True)  36.9 us
    unnamed x30, local copies, waits for them, and re-layouts  17.7 us
  transfers between devices with their start and end apart: 20, of which 19 were waited for; matrix products, arithmetic and copies ran while one was open for 1% of the time, Pallas kernels for 17%

profile of v1, /device:TPU:0, one launch (start us, length us, event | category | flops | bytes accessed | tf_op | source)
XLA Modules:
  0.0 700.6 jit_solution(4650201999786654307)
XLA Ops:
  7.2 1.9 fusion.36
  11.7 29.1 %all-gather.11.cloned.1.call-done.x_ref = bf16[256,2048]{1,0:T(8,128)(2,1)} async-done(((bf16[64,2048]{1,0:T(8,128)(2,1)}), bf16[256,2048]{1,0:T(8,128)(2,1)}) %all-gather.11.cloned.1.call-update) | async-done | bytes 1048592 | tf_op jit(solution)/shard_map/all_gather | solution.py:132
  42.0 13.3 %shard_map.77 = (bf16[256,3072]{1,0:T(8,128)(2,1)}, bf16[256,3072]{1,0:T(8,128)(2,1)}) custom-call(bf16[256,2048]{1,0:T(8,128)(2,1)S(1)} %copy-done.4, bf16[2048,6656]{1,0:T(8,128)(2,1)} %wg_ref.15, bf16[2048,6656]{1,0:T(8,128)(2,1)} %wu_ref.15, bf16[16,6656]{1,0:T(8,128)(2,1)S(1)} %get-tuple-element.37.fg_ref, bf16[16,6656]{1,0:T(8,128)(2,1)S(1)} %get-tuple-element.36.fu_ref), custom_call_target="tpu_custom_call" | custom-call | flops 6442450944 | bytes 29360128 | tf_op jit(solution)/shard_map/pallas_call | solution.py:40
  56.0 14.4 %all-gather.13.cloned.1.call-done.x_ref = bf16[256,2048]{1,0:T(8,128)(2,1)} async-done(((bf16[64,2048]{1,0:T(8,128)(2,1)}), bf16[256,2048]{1,0:T(8,128)(2,1)}) %all-gather.13.cloned.1.call-update) | async-done | bytes 1048592 | tf_op jit(solution)/shard_map/all_gather | solution.py:132
  71.6 13.6 %shard_map.79 = (bf16[256,3072]{1,0:T(8,128)(2,1)}, bf16[256,3072]{1,0:T(8,128)(2,1)}) custom-call(bf16[256,2048]{1,0:T(8,128)(2,1)S(1)} %copy-done.2, bf16[2048,6656]{1,0:T(8,128)(2,1)} %wg_ref.15, bf16[2048,6656]{1,0:T(8,128)(2,1)} %wu_ref.15, bf16[16,6656]{1,0:T(8,128)(2,1)S(1)} %get-tuple-element.37.fg_ref, bf16[16,6656]{1,0:T(8,128)(2,1)S(1)} %get-tuple-element.36.fu_ref), custom_call_target="tpu_custom_call" | custom-call | flops 6442450944 | bytes 29360128 | tf_op jit(solution)/shard_map/pallas_call | solution.py:40
  86.5 15.7 %shard_map.78 = (bf16[256,3584]{1,0:T(8,128)(2,1)}, bf16[256,3584]{1,0:T(8,128)(2,1)}) custom-call(bf16[256,2048]{1,0:T(8,128)(2,1)S(1)} %copy-done.5, bf16[2048,6656]{1,0:T(8,128)(2,1)} %wg_ref.15, bf16[2048,6656]{1,0:T(8,128)(2,1)} %wu_ref.15, bf16[16,6656]{1,0:T(8,128)(2,1)S(1)} %get-tuple-element.37.fg_ref, bf16[16,6656]{1,0:T(8,128)(2,1)S(1)} %get-tuple-element.36.fu_ref), custom_call_target="tpu_custom_call" | custom-call | flops 7516192768 | bytes 34078720 | tf_op jit(solution)/shard_map/pallas_call | solution.py:40
  103.4 15.7 %shard_map.80 = (bf16[256,3584]{1,0:T(8,128)(2,1)}, bf16[256,3584]{1,0:T(8,128)(2,1)}) custom-call(bf16[256,2048]{1,0:T(8,128)(2,1)S(1)} %copy-done.3, bf16[2048,6656]{1,0:T(8,128)(2,1)} %wg_ref.15, bf16[2048,6656]{1,0:T(8,128)(2,1)} %wu_ref.15, bf16[16,6656]{1,0:T(8,128)(2,1)S(1)} %get-tuple-element.37.fg_ref, bf16[16,6656]{1,0:T(8,128)(2,1)S(1)} %get-tuple-element.36.fu_ref), custom_call_target="tpu_custom_call" | custom-call | flops 7516192768 | bytes 34078720 | tf_op jit(solution)/shard_map/pallas_call | solution.py:40
  119.8 33.5 %reduce-scatter.13.cloned.1.call-done = bf16[32,3072]{1,0:T(8,128)(2,1)} async-done(((bf16[256,3072]{1,0:T(8,128)(2,1)}), bf16[32,3072]{1,0:T(8,128)(2,1)}) %reduce-scatter.13.cloned.1.call-update) | async-done | bytes 196624 | tf_op jit(solution)/shard_map/reduce_scatter | solution.py:142
  153.4 41.6 %reduce-scatter.19.cloned.1.call-done = bf16[32,3072]{1,0:T(8,128)(2,1)} async-done(((bf16[256,3072]{1,0:T(8,128)(2,1)}), bf16[32,3072]{1,0:T(8,128)(2,1)}) %reduce-scatter.19.cloned.1.call-update) | async-done | bytes 196624 | tf_op jit(solution)/shard_map/reduce_scatter | solution.py:142
  195.0 41.6 %reduce-scatter.21.cloned.1.call-done = bf16[32,3072]{1,0:T(8,128)(2,1)} async-done(((bf16[256,3072]{1,0:T(8,128)(2,1)}), bf16[32,3072]{1,0:T(8,128)(2,1)}) %reduce-scatter.21.cloned.1.call-update) | async-done | bytes 196624 | tf_op jit(solution)/shard_map/reduce_scatter | solution.py:142
  236.6 2.5 fusion.23
  239.8 39.9 %reduce-scatter.15.cloned.1.call-done = bf16[32,3584]{1,0:T(8,128)(2,1)} async-done(((bf16[256,3584]{1,0:T(8,128)(2,1)}), bf16[32,3584]{1,0:T(8,128)(2,1)}) %reduce-scatter.15.cloned.1.call-update) | async-done | bytes 229392 | tf_op jit(solution)/shard_map/reduce_scatter | solution.py:142
  279.7 43.1 %reduce-scatter.17.cloned.1.call-done = bf16[32,3584]{1,0:T(8,128)(2,1)} async-done(((bf16[256,3584]{1,0:T(8,128)(2,1)}), bf16[32,3584]{1,0:T(8,128)(2,1)}) %reduce-scatter.17.cloned.1.call-update) | async-done | bytes 229392 | tf_op jit(solution)/shard_map/reduce_scatter | solution.py:142
  322.7 43.1 %reduce-scatter.23.cloned.1.call-done = bf16[32,3584]{1,0:T(8,128)(2,1)} async-done(((bf16[256,3584]{1,0:T(8,128)(2,1)}), bf16[32,3584]{1,0:T(8,128)(2,1)}) %reduce-scatter.23.cloned.1.call-update) | async-done | bytes 229392 | tf_op jit(solution)/shard_map/reduce_scatter | solution.py:142
  365.8 42.9 %reduce-scatter.25.cloned.1.call-done = bf16[32,3584]{1,0:T(8,128)(2,1)} async-done(((bf16[256,3584]{1,0:T(8,128)(2,1)}), bf16[32,3584]{1,0:T(8,128)(2,1)}) %reduce-scatter.25.cloned.1.call-update) | async-done | bytes 229392 | tf_op jit(solution)/shard_map/reduce_scatter | solution.py:142
  408.7 2.7 fusion.5
  414.4 22.0 %all-gather.23.cloned.1.call-done.gg_ref = bf16[256,3072]{1,0:T(8,128)(2,1)} async-done(((bf16[32,3072]{1,0:T(8,128)(2,1)}), bf16[256,3072]{1,0:T(8,128)(2,1)}) %all-gather.23.cloned.1.call-update) | async-done | bytes 1572880 | tf_op jit(solution)/shard_map/all_gather | solution.py:154
  436.4 27.5 %all-gather.25.cloned.1.call-done.gu_ref = bf16[256,3072]{1,0:T(8,128)(2,1)} async-done(((bf16[32,3072]{1,0:T(8,128)(2,1)}), bf16[256,3072]{1,0:T(8,128)(2,1)}) %all-gather.25.cloned.1.call-update) | async-done | bytes 1572880 | tf_op jit(solution)/shard_map/all_gather | solution.py:154
  466.6 12.9 %shard_map.83.a_ref = f32[256,2048]{1,0:T(8,128)S(1)} custom-call(bf16[256,3072]{1,0:T(8,128)(2,1)S(1)} %copy-done.10, bf16[256,3072]{1,0:T(8,128)(2,1)S(1)} %copy-done.11, bf16[2048,6656]{1,0:T(8,128)(2,1)} %wg_ref.15, bf16[2048,6656]{1,0:T(8,128)(2,1)} %wu_ref.15, bf16[16,6656]{1,0:T(8,128)(2,1)S(1)} %get-tuple-element.37.fg_ref, ...), custom_call_target="tpu_custom_call" | custom-call | flops 6442450944 | bytes 29360128 | tf_op jit(solution)/shard_map/pallas_call | solution.py:87
  480.8 11.7 %all-gather.27.cloned.1.call-done.gg_ref = bf16[256,3584]{1,0:T(8,128)(2,1)} async-done(((bf16[32,3584]{1,0:T(8,128)(2,1)}), bf16[256,3584]{1,0:T(8,128)(2,1)}) %all-gather.27.cloned.1.call-update) | async-done | bytes 1835024 | tf_op jit(solution)/shard_map/all_gather | solution.py:154
  492.5 28.6 %all-gather.29.cloned.1.call-done.gu_ref = bf16[256,3584]{1,0:T(8,128)(2,1)} async-done(((bf16[32,3584]{1,0:T(8,128)(2,1)}), bf16[256,3584]{1,0:T(8,128)(2,1)}) %all-gather.29.cloned.1.call-update) | async-done | bytes 1835024 | tf_op jit(solution)/shard_map/all_gather | solution.py:154
  521.1 1.5 copy-done.6
  522.6 1.5 copy-done.8
  524.1 16.5 %shard_map.84 = bf16[256,2048]{1,0:T(8,128)(2,1)} custom-call(f32[256,2048]{1,0:T(8,128)} %copy-done.1, bf16[256,3584]{1,0:T(8,128)(2,1)S(1)} %copy-done.6, bf16[256,3584]{1,0:T(8,128)(2,1)S(1)} %copy-done.8, bf16[2048,6656]{1,0:T(8,128)(2,1)} %wg_ref.15, bf16[2048,6656]{1,0:T(8,128)(2,1)} %wu_ref.15, bf16[16,6656]{1,0:T(8,128)(2,1)S(1)} %get-tuple-element.37.fg_ref, ...), custom_call_target="tpu_custom_call" | custom-call | flops 7516192768 | bytes 34078720 | tf_op jit(solution)/shard_map/pallas_call | solution.py:87
  540.9 7.7 %all-gather.15.cloned.1.call-done.gg_ref = bf16[256,3072]{1,0:T(8,128)(2,1)} async-done(((bf16[32,3072]{1,0:T(8,128)(2,1)}), bf16[256,3072]{1,0:T(8,128)(2,1)}) %all-gather.15.cloned.1.call-update) | async-done | bytes 1572880 | tf_op jit(solution)/shard_map/all_gather | solution.py:154
  548.6 27.5 %all-gather.17.cloned.1.call-done.gu_ref = bf16[256,3072]{1,0:T(8,128)(2,1)} async-done(((bf16[32,3072]{1,0:T(8,128)(2,1)}), bf16[256,3072]{1,0:T(8,128)(2,1)}) %all-gather.17.cloned.1.call-update) | async-done | bytes 1572880 | tf_op jit(solution)/shard_map/all_gather | solution.py:154
  578.8 12.9 %shard_map.81.a_ref = f32[256,2048]{1,0:T(8,128)S(1)} custom-call(bf16[256,3072]{1,0:T(8,128)(2,1)S(1)} %copy-done.12, bf16[256,3072]{1,0:T(8,128)(2,1)S(1)} %copy-done.13, bf16[2048,6656]{1,0:T(8,128)(2,1)} %wg_ref.15, bf16[2048,6656]{1,0:T(8,128)(2,1)} %wu_ref.15, bf16[16,6656]{1,0:T(8,128)(2,1)S(1)} %get-tuple-element.37.fg_ref, ...), custom_call_target="tpu_custom_call" | custom-call | flops 6442450944 | bytes 29360128 | tf_op jit(solution)/shard_map/pallas_call | solution.py:87
  593.1 12.1 %all-gather.19.cloned.1.call-done.gg_ref = bf16[256,3584]{1,0:T(8,128)(2,1)} async-done(((bf16[32,3584]{1,0:T(8,128)(2,1)}), bf16[256,3584]{1,0:T(8,128)(2,1)}) %all-gather.19.cloned.1.call-update) | async-done | bytes 1835024 | tf_op jit(solution)/shard_map/all_gather | solution.py:154
  605.2 29.1 %all-gather.21.cloned.1.call-done.gu_ref = bf16[256,3584]{1,0:T(8,128)(2,1)} async-done(((bf16[32,3584]{1,0:T(8,128)(2,1)}), bf16[256,3584]{1,0:T(8,128)(2,1)}) %all-gather.21.cloned.1.call-update) | async-done | bytes 1835024 | tf_op jit(solution)/shard_map/all_gather | solution.py:154
  637.3 16.7 %shard_map.82 = bf16[256,2048]{1,0:T(8,128)(2,1)} custom-call(f32[256,2048]{1,0:T(8,128)} %copy-done, bf16[256,3584]{1,0:T(8,128)(2,1)S(1)} %copy-done.7, bf16[256,3584]{1,0:T(8,128)(2,1)S(1)} %copy-done.9, bf16[2048,6656]{1,0:T(8,128)(2,1)} %wg_ref.15, bf16[2048,6656]{1,0:T(8,128)(2,1)} %wu_ref.15, bf16[16,6656]{1,0:T(8,128)(2,1)S(1)} %get-tuple-element.37.fg_ref, ...), custom_call_target="tpu_custom_call" | custom-call | flops 7516192768 | bytes 34078720 | tf_op jit(solution)/shard_map/pallas_call | solution.py:87
  654.9 8.8 %reduce-scatter.29.cloned.1.call-done = bf16[64,2048]{1,0:T(8,128)(2,1)} async-done(((bf16[256,2048]{1,0:T(8,128)(2,1)}), bf16[64,2048]{1,0:T(8,128)(2,1)}) %reduce-scatter.29.cloned.1.call-update) | async-done | bytes 262160 | tf_op jit(solution)/shard_map/reduce_scatter | solution.py:167
  663.8 28.1 %reduce-scatter.27.cloned.1.call-done = bf16[64,2048]{1,0:T(8,128)(2,1)} async-done(((bf16[256,2048]{1,0:T(8,128)(2,1)}), bf16[64,2048]{1,0:T(8,128)(2,1)}) %reduce-scatter.27.cloned.1.call-update) | async-done | bytes 262160 | tf_op jit(solution)/shard_map/reduce_scatter | solution.py:167
  (77 shorter events, 26.6 us)
Async XLA Ops:
  7.2 33.6 %all-gather.11.cloned.1.call-start = ((), (), s32[]{:S(2)}) async-start(), calls=%async_computation.10 | async-start | bytes 1310720 | tf_op jit(solution)/shard_map/all_gather | solution.py:132
  9.1 61.3 %all-gather.13.cloned.1.call-start = ((), (), s32[]{:S(2)}) async-start(), calls=%async_computation.15 | async-start | bytes 1310720 | tf_op jit(solution)/shard_map/all_gather | solution.py:132
  9.9 110.0 %reduce-scatter.11.cloned.1.call-start = ((), (), s32[]{:S(2)}) async-start(), calls=%async_computation.11 | async-start | bytes 1769472 | tf_op jit(solution)/shard_map/reduce_scatter | solution.py:142
  55.4 98.0 %reduce-scatter.13.cloned.1.call-start = ((), (), s32[]{:S(2)}) async-start(), calls=%async_computation.12 | async-start | bytes 1769472 | tf_op jit(solution)/shard_map/reduce_scatter | solution.py:142
  56.0 139.0 %reduce-scatter.19.cloned.1.call-start = ((), (), s32[]{:S(2)}) async-start(), calls=%async_computation.16 | async-start | bytes 1769472 | tf_op jit(solution)/shard_map/reduce_scatter | solution.py:142
  85.2 1.2 copy-start.5
  85.2 151.4 %reduce-scatter.21.cloned.1.call-start = ((), (), s32[]{:S(2)}) async-start(), calls=%async_computation.17 | async-start | bytes 1769472 | tf_op jit(solution)/shard_map/reduce_scatter | solution.py:142
  85.8 193.9 %reduce-scatter.15.cloned.1.call-start = ((), (), s32[]{:S(2)}) async-start(), calls=%async_computation.13 | async-start | bytes 2064384 | tf_op jit(solution)/shard_map/reduce_scatter | solution.py:142
  102.2 220.5 %reduce-scatter.17.cloned.1.call-start = ((), (), s32[]{:S(2)}) async-start(), calls=%async_computation.14 | async-start | bytes 2064384 | tf_op jit(solution)/shard_map/reduce_scatter | solution.py:142
  103.0 262.9 %reduce-scatter.23.cloned.1.call-start = ((), (), s32[]{:S(2)}) async-start(), calls=%async_computation.18 | async-start | bytes 2064384 | tf_op jit(solution)/shard_map/reduce_scatter | solution.py:142
  119.1 117.5 %copy-start.14 = (bf16[64,6656]{1,0:T(8,128)(2,1)S(1)}, bf16[64,6656]{1,0:T(8,128)(2,1)}, u32[]{:S(2)}) copy-start(bf16[64,6656]{1,0:T(8,128)(2,1)} %param.11) | copy-start | bytes 2555908
  119.2 289.6 %reduce-scatter.25.cloned.1.call-start = ((), (), s32[]{:S(2)}) async-start(), calls=%async_computation.19 | async-start | bytes 2064384 | tf_op jit(solution)/shard_map/reduce_scatter | solution.py:142
  119.8 316.6 %all-gather.23.cloned.1.call-start = ((), (), s32[]{:S(2)}) async-start(), calls=%async_computation.25 | async-start | bytes 1769472 | tf_op jit(solution)/shard_map/all_gather | solution.py:154
  239.2 224.7 %all-gather.25.cloned.1.call-start = ((), (), s32[]{:S(2)}) async-start(), calls=%async_computation.26 | async-start | bytes 1769472 | tf_op jit(solution)/shard_map/all_gather | solution.py:154
  239.7 252.8 %all-gather.27.cloned.1.call-start = ((), (), s32[]{:S(2)}) async-start(), calls=%async_computation.27 | async-start | bytes 2064384 | tf_op jit(solution)/shard_map/all_gather | solution.py:154
  411.4 109.7 %all-gather.29.cloned.1.call-start = ((), (), s32[]{:S(2)}) async-start(), calls=%async_computation.28 | async-start | bytes 2064384 | tf_op jit(solution)/shard_map/all_gather | solution.py:154
  412.0 136.5 %all-gather.15.cloned.1.call-start = ((), (), s32[]{:S(2)}) async-start(), calls=%async_computation.20 | async-start | bytes 1769472 | tf_op jit(solution)/shard_map/all_gather | solution.py:154
  412.6 163.4 %all-gather.17.cloned.1.call-start = ((), (), s32[]{:S(2)}) async-start(), calls=%async_computation.21 | async-start | bytes 1769472 | tf_op jit(solution)/shard_map/all_gather | solution.py:154
  413.2 192.0 %all-gather.19.cloned.1.call-start = ((), (), s32[]{:S(2)}) async-start(), calls=%async_computation.22 | async-start | bytes 2064384 | tf_op jit(solution)/shard_map/all_gather | solution.py:154
  413.8 220.5 %all-gather.21.cloned.1.call-start = ((), (), s32[]{:S(2)}) async-start(), calls=%async_computation.23 | async-start | bytes 2064384 | tf_op jit(solution)/shard_map/all_gather | solution.py:154
  414.4 249.4 %reduce-scatter.29.cloned.1.call-start = ((), (), s32[]{:S(2)}) async-start(), calls=%async_computation.29 | async-start | bytes 1310720 | tf_op jit(solution)/shard_map/reduce_scatter | solution.py:167
  463.8 1.4 copy-start.10
  465.2 1.4 copy-start.11
  479.5 1.3 copy-start.1
  521.1 1.5 copy-start.6
  522.6 1.5 copy-start.8
  540.7 151.2 %reduce-scatter.27.cloned.1.call-start = ((), (), s32[]{:S(2)}) async-start(), calls=%async_computation.24 | async-start | bytes 1310720 | tf_op jit(solution)/shard_map/reduce_scatter | solution.py:167
  576.0 1.4 copy-start.12
  577.4 1.4 copy-start.13
  591.7 1.3 copy-start
  634.3 1.5 copy-start.7
  635.8 1.5 copy-start.9
  (3 other events, 3.7 us)
Sparse Core Ops, SparseCore 0:
  10.1 30.6 all-gather.10
  42.9 27.4 all-gather.12
  73.7 37.9 reduce-scatter.10
  114.9 38.4 reduce-scatter.12
  156.5 38.4 reduce-scatter.18
  198.1 38.4 reduce-scatter.20
  240.0 39.6 reduce-scatter.14
  283.0 39.6 reduce-scatter.16
  326.1 39.6 reduce-scatter.22
  369.0 39.6 reduce-scatter.24
  410.6 25.6 all-gather.22
  438.1 25.6 all-gather.24
  465.7 26.7 all-gather.26
  494.3 26.7 all-gather.28
  522.8 25.6 all-gather.14
  550.3 25.6 all-gather.16
  578.3 26.7 all-gather.18
  607.5 26.7 all-gather.20
  636.6 27.1 reduce-scatter.28
  666.0 25.7 reduce-scatter.26

commit v2 on v1

v2 whole, which is shorter than its diff:
```python
import functools

import jax
import jax.numpy as jnp
import numpy as np
from jax import lax
from jax.experimental import pallas as pl
from jax.experimental.pallas import tpu as pltpu
from jax.sharding import PartitionSpec as P

BLOCK = 128
TOKEN_CHUNKS = 2
FORWARD_CHUNKS = 4
GROUP = 2
VMEM_BYTES = 48 * 1024 * 1024
ANY = pl.BlockSpec(memory_space=pl.ANY)


def masked(w_ref, f_ref):
    return jnp.concatenate(
        [
            w_ref[k * BLOCK : (k + 1) * BLOCK, :] * f_ref[k : k + 1, :]
            for k in range(w_ref.shape[0] // BLOCK)
        ],
        axis=0,
    )


class Cube:
    def __init__(self, size):
        self.size = size
        self.half = size // 2
        rising = [1 << b for b in range(1, size.bit_length() - 1)]
        self.dims = (rising, rising[::-1])

    def offset(self, parity, slot):
        dims = self.dims[parity]
        digits = [slot >> (len(dims) - 1 - i) & 1 for i in range(len(dims))]
        return int(np.bitwise_xor.reduce([0] + [d for d, on in zip(dims, digits) if on]))

    def owner(self, me, slot):
        if slot >= self.half:
            me, slot = me ^ 1, slot - self.half
        return me ^ self.offset(me & 1, slot)

    def step(self, array, i):
        perm = [(r, r ^ self.dims[r & 1][i]) for r in range(self.size)]
        return lax.ppermute(array, "row", perm)

    def sibling(self, array):
        return lax.ppermute(array, "row", [(r, r ^ 1) for r in range(self.size)])


def places(cube, n_col):
    ratio = cube.size // n_col
    table = np.zeros((cube.size, n_col, cube.size), np.int32)
    for me in range(cube.size):
        for z in range(n_col):
            for slot in range(cube.size):
                d = cube.owner(me, slot)
                table[me, z, slot] = ratio * ((d // ratio) ^ z) + d % ratio
    return table


def forward_kernel(n_x, slots, *refs):
    x_refs = refs[:n_x]
    wg_ref, wu_ref, fg_ref, fu_ref, keep_ref, send_ref, x_all, sem = refs[n_x:]
    half = keep_ref.shape[1]
    shares = slots.shape[0]
    share = 2 * half // shares
    ratio = shares // n_x

    @pl.when(pl.program_id(0) == 0)
    def _():
        copies = []
        for k in range(n_x):
            for c in range(ratio):
                place = k * ratio + c
                row = pl.multiple_of(slots[place] * share, share)
                copies.append(
                    pltpu.make_async_copy(
                        x_refs[k].at[pl.ds(c * share, share), :],
                        x_all.at[pl.ds(row, share), :],
                        sem.at[place],
                    )
                )
        for copy in copies:
            copy.start()
        for copy in copies:
            copy.wait()

    for n, (w_ref, f_ref) in enumerate(((wg_ref, fg_ref), (wu_ref, fu_ref))):
        out = jnp.dot(
            x_all[...], masked(w_ref, f_ref), preferred_element_type=jnp.float32
        ).astype(jnp.bfloat16)
        keep_ref[n] = out[:half]
        send_ref[n] = out[half:]


def forward(slots, xs, weights, flags, first, tiles, tile):
    depth = xs[0].shape[1]
    rows = len(xs) * xs[0].shape[0]
    blocks = flags[0].shape[0]
    w_spec = pl.BlockSpec((depth, tile), lambda i, s: (0, first + i))
    f_spec = pl.BlockSpec((blocks, tile), lambda i, s: (0, first + i))
    o_spec = pl.BlockSpec((2, rows // 2, tile), lambda i, s: (0, 0, i))
    out = jax.ShapeDtypeStruct((2, rows // 2, tiles * tile), jnp.bfloat16)
    return pl.pallas_call(
        functools.partial(forward_kernel, len(xs)),
        grid_spec=pltpu.PrefetchScalarGridSpec(
            num_scalar_prefetch=1,
            grid=(tiles,),
            in_specs=[ANY] * len(xs) + [w_spec, w_spec, f_spec, f_spec],
            out_specs=[o_spec, o_spec],
            scratch_shapes=[
                pltpu.VMEM((rows, depth), jnp.bfloat16),
                pltpu.SemaphoreType.DMA((slots.shape[0],)),
            ],
        ),
        out_shape=[out, out],
        compiler_params=pltpu.CompilerParams(vmem_limit_bytes=VMEM_BYTES),
        cost_estimate=pl.CostEstimate(
            flops=4 * rows * depth * tiles * tile,
            bytes_accessed=4 * tiles * tile * (depth + rows) + 2 * rows * depth,
            transcendentals=0,
        ),
    )(slots, *xs, *weights, *flags)


def backward_kernel(n_g, n_out, steps, chained, where, *refs):
    g_refs, refs = refs[:n_g], refs[n_g:]
    wg_ref, wu_ref, fg_ref, fu_ref = refs[:4]
    refs = refs[4:]
    if chained:
        carry_ref, refs = refs[0], refs[1:]
    o_refs = refs[:n_out]
    g_all, acc, sem = refs[n_out:]
    i = pl.program_id(0)
    tile = wg_ref.shape[1]
    share = g_refs[0].shape[1]

    @pl.when(i == 0)
    def _():
        copies = []
        for slot in range(n_g):
            row = pl.multiple_of(where[slot] * share, share)
            copies.append(
                pltpu.make_async_copy(
                    g_refs[slot], g_all.at[:, pl.ds(row, share), :], sem.at[slot]
                )
            )
        for copy in copies:
            copy.start()
        if chained:
            acc[...] = carry_ref[...]
        else:
            acc[...] = jnp.zeros_like(acc)
        for copy in copies:
            copy.wait()

    columns = pl.ds(pl.multiple_of(i * tile, tile), tile)
    for n, (w_ref, f_ref) in enumerate(((wg_ref, fg_ref), (wu_ref, fu_ref))):
        acc[...] += lax.dot_general(
            masked(w_ref, f_ref),
            g_all[n, :, columns],
            (((1,), (1,)), ((), ())),
            preferred_element_type=jnp.float32,
        )

    @pl.when(i == steps - 1)
    def _():
        if n_out == 1:
            o_refs[0][...] = acc[...]
        else:
            out = acc[...].T.astype(jnp.bfloat16)
            rows = out.shape[0] // n_out
            for k in range(n_out):
                o_refs[k][...] = out[k * rows : (k + 1) * rows]


def backward(carry, where, pieces, weights, flags, first, tiles, tile, planes):
    share = pieces[0].shape[1]
    rows = share * len(pieces)
    blocks = flags[0].shape[0]
    depth = weights[0].shape[0]
    w_spec = pl.BlockSpec((depth, tile), lambda i, s: (0, first + i))
    f_spec = pl.BlockSpec((blocks, tile), lambda i, s: (0, first + i))
    whole = pl.BlockSpec((depth, rows), lambda i, s: (0, 0))
    if planes:
        out_specs = [pl.BlockSpec((rows // planes, depth), lambda i, s: (0, 0))] * planes
        out_shape = [jax.ShapeDtypeStruct((rows // planes, depth), jnp.bfloat16)] * planes
    else:
        out_specs = [whole]
        out_shape = [jax.ShapeDtypeStruct((depth, rows), jnp.float32)]
    chained = carry is not None
    return pl.pallas_call(
        functools.partial(backward_kernel, len(pieces), len(out_shape), tiles, chained),
        grid_spec=pltpu.PrefetchScalarGridSpec(
            num_scalar_prefetch=1,
            grid=(tiles,),
            in_specs=[ANY] * len(pieces)
            + [w_spec, w_spec, f_spec, f_spec]
            + [whole] * chained,
            out_specs=out_specs,
            scratch_shapes=[
                pltpu.VMEM((2, rows, tiles * tile), jnp.bfloat16),
                pltpu.VMEM((depth, rows), jnp.float32),
                pltpu.SemaphoreType.DMA((len(pieces),)),
            ],
        ),
        out_shape=out_shape,
        compiler_params=pltpu.CompilerParams(vmem_limit_bytes=VMEM_BYTES),
        cost_estimate=pl.CostEstimate(
            flops=4 * rows * depth * tiles * tile,
            bytes_accessed=4 * tiles * tile * (depth + rows) + 2 * rows * depth,
            transcendentals=0,
        ),
    )(where, *pieces, *weights, *flags, *((carry,) if chained else ()))


def wide(array):
    return array.astype(jnp.float32)


def reduce_scatter(cube, keep, send):
    terms = [keep, cube.sibling(send)]
    rows = keep.shape[1]
    for i in range(len(cube.dims[0])):
        rows //= 2
        moved = sum(wide(t[:, rows : 2 * rows]) for t in terms).astype(jnp.bfloat16)
        terms = [t[:, :rows] for t in terms] + [cube.step(moved, i)]
    return sum(wide(t) for t in terms)


def all_gather(cube, own):
    n_dims = len(cube.dims[0])
    pieces = [own]
    for slot in range(1, cube.half):
        low = slot & -slot
        pieces.append(cube.step(pieces[slot ^ low], n_dims - low.bit_length()))
    return pieces + [cube.sibling(p) for p in pieces]


def flip(array, bit, size):
    return lax.ppermute(array, "col", [(z, z ^ bit) for z in range(size)])


def derivatives(gate_sum, up_sum, cotangent):
    sigmoid_gate = jax.nn.sigmoid(gate_sum)
    activated = gate_sum * sigmoid_gate
    hidden = (activated * up_sum).astype(jnp.bfloat16)
    cotangent_f = wide(cotangent)
    gate_grad = (
        cotangent_f * up_sum * sigmoid_gate * (1.0 + gate_sum * (1.0 - sigmoid_gate))
    ).astype(jnp.bfloat16)
    up_grad = (cotangent_f * activated).astype(jnp.bfloat16)
    return hidden, gate_grad, up_grad


def shards(cube, n_col, inputs, gate_weight, up_weight, gate_pattern, up_pattern, cotangent):
    depth, local_hidden = gate_weight.shape
    share = cotangent.shape[0]
    piece = share // TOKEN_CHUNKS
    tile = 512 if local_hidden % 512 == 0 else 256
    n_tiles = local_hidden // tile
    bounds = [n_tiles * c // FORWARD_CHUNKS for c in range(FORWARD_CHUNKS + 1)]
    weights = (gate_weight, up_weight)
    flags = tuple(
        jnp.repeat(p.astype(jnp.bfloat16), BLOCK, axis=1) for p in (gate_pattern, up_pattern)
    )
    table = places(cube, n_col)
    row, col = lax.axis_index("row"), lax.axis_index("col")
    where = jnp.asarray(table)[row, col]
    slots = jnp.asarray(np.argsort(table, axis=-1).astype(np.int32))[row, col]

    xs = [inputs]
    for k in range(1, n_col):
        low = k & -k
        xs.append(flip(xs[k ^ low], low, n_col))

    sums = []
    for c in range(FORWARD_CHUNKS):
        keep, send = forward(
            slots, xs, weights, flags, bounds[c], bounds[c + 1] - bounds[c], tile
        )
        sums.append(reduce_scatter(cube, keep, send))

    hidden, input_grad = [], []
    for t in range(TOKEN_CHUNKS):
        rows = slice(t * piece, (t + 1) * piece)
        hidden_row = []
        carry = None
        for c in range(0, FORWARD_CHUNKS, GROUP):
            last = c + GROUP == FORWARD_CHUNKS
            results = [
                derivatives(
                    sums[b][0, rows],
                    sums[b][1, rows],
                    cotangent[rows, bounds[b] * tile : bounds[b + 1] * tile],
                )
                for b in range(c, c + GROUP)
            ]
            hidden_row += [r[0] for r in results]
            own = jnp.stack(
                [jnp.concatenate([r[n] for r in results], axis=1) for n in (1, 2)]
            )
            parts = backward(
                carry,
                where,
                all_gather(cube, own),
                weights,
                flags,
                bounds[c],
                bounds[c + GROUP] - bounds[c],
                tile,
                n_col if last else 0,
            )
            carry = parts[0]
        hidden.append(jnp.concatenate(hidden_row, axis=1))
        parts = list(parts)
        for k in range(n_col - 1, 0, -1):
            low = k & -k
            moved = flip(parts[k].astype(jnp.bfloat16), low, n_col)
            parts[k ^ low] = wide(parts[k ^ low]) + wide(moved)
        input_grad.append(parts[0].astype(jnp.bfloat16).reshape(-1, 1, piece, depth))
    return (
        jnp.concatenate(hidden, axis=0),
        jnp.concatenate(input_grad, axis=1).reshape(-1, depth),
    )


def solution(mesh):
    placed = (
        P("col", "row"),
        P("row", "col"),
        P("row", "col"),
        P("row", "col"),
        P("row", "col"),
        P("row", "col"),
    )
    return jax.shard_map(
        functools.partial(shards, Cube(mesh.shape["row"]), mesh.shape["col"]),
        mesh=mesh,
        in_specs=placed,
        out_specs=(P("row", "col"), P("col", "row")),
        check_vma=False,
    )
```

time: 701 us -> 288 us (0.41)
  waiting for transfers between devices: 538 us -> 112 us
  starting transfers between devices: 0.97 us -> 45.7 us
  local copies, waits for them, and re-layouts: 20.8 us -> 5.34 us
  between operations: 14.4 us -> 1.02 us
  Pallas kernels: 117 us -> 108 us
  other arithmetic: 8.61 us -> 16.3 us
    reduce_scatter x10 -> x0, waiting for transfers between devices: 323 us -> none  [the longest x8 286 us: shards(): lax.psum_scatter(p, 'row', scatter_dimension=0, tiled=True)]
    all_gather x10 -> x0, waiting for transfers between devices: 210 us -> none  [the longest x8 166 us: shards(): lax.all_gather(g, 'row', axis=0, tiled=True)]
    ppermute x0 -> x49, waiting for transfers between devices: none -> 112 us  [the longest x9 56.3 us: flip(): return lax.ppermute(array, 'col', [(z, z ^ bit) for z in range(size)])]
    ppermute x0 -> x49, starting transfers between devices: none -> 45.7 us  [the longest x20 24.6 us: step(): return lax.ppermute(array, 'row', perm)]
    unnamed x30 -> x8, local copies, waits for them, and re-layouts: 17.7 us -> 2.72 us
    pallas_call x8, Pallas kernels: 117 us -> 108 us  [the longest x4 63.2 us: backward(): pl.pallas_call(functools.partial(backward_kernel, len(pieces), len(out_sh...]
  transfers between devices with their start and end apart: 20 -> 49, of which waited for: 19 -> 15; matrix products, arithmetic and copies ran while one was open for 1% -> 6% of each run, Pallas kernels for 17% -> 34%
where the time goes in v2:
time: 288 us
  waiting for transfers between devices  112 us (39%)
  Pallas kernels  108 us (38%)
  starting transfers between devices  45.7 us (16%)
  other arithmetic  16.3 us (6%)
  local copies, waits for them, and re-layouts  5.34 us (2%)
    pallas_call x4, Pallas kernels, backward(): pl.pallas_call(functools.partial(backward_kernel, len(pieces), len(out_sh...  63.2 us
    ppermute x9, waiting for transfers between devices, flip(): return lax.ppermute(array, 'col', [(z, z ^ bit) for z in range(size)])  56.3 us
    ppermute x20, waiting for transfers between devices, step(): return lax.ppermute(array, 'row', perm)  55.3 us
    pallas_call x4, Pallas kernels, forward(): pl.pallas_call(functools.partial(forward_kernel, len(xs)), grid_spec=pltp...  44.3 us
    ppermute x20, starting transfers between devices, step(): return lax.ppermute(array, 'row', perm)  24.6 us
    ppermute x9, starting transfers between devices, flip(): return lax.ppermute(array, 'col', [(z, z ^ bit) for z in range(size)])  16.5 us
    convert_element_type x8, other arithmetic, reduce_scatter(): moved = sum((wide(t[:, rows:2 * rows]) for t in terms)).astype(jnp.bfloat16)  8.24 us
  transfers between devices with their start and end apart: 49, of which 15 were waited for; matrix products, arithmetic and copies ran while one was open for 6% of the time, Pallas kernels for 34%

profile of v2, /device:TPU:0, one launch (start us, length us, event | category | flops | bytes accessed | tf_op | source)
XLA Modules:
  0.0 287.6 jit_solution(5956492083650662787)
XLA Ops:
  0.6 4.1 %collective-permute-start.1 = (bf16[128,2048]{1,0:T(8,128)(2,1)}, bf16[128,2048]{1,0:T(8,128)(2,1)S(1)}, u32[]{:S(2)}, u32[]{:S(2)}) collective-permute-start(bf16[128,2048]{1,0:T(8,128)(2,1)} %refs_0_.7), channel_id=1, source_target_pairs={{0,2},{1,3},{2,0},{3,1},{4,6},{5,7},{6,4},{7,5},{8,10},{9,11},{10,... | collective-permute-start | bytes 1572872 | tf_op jit(solution)/shard_map/ppermute | solution.py:245
  4.7 1.6 collective-permute-start
  7.7 20.5 %collective-permute-done.1.refs_2_ = bf16[128,2048]{1,0:T(8,128)(2,1)S(1)} collective-permute-done((bf16[128,2048]{1,0:T(8,128)(2,1)}, bf16[128,2048]{1,0:T(8,128)(2,1)S(1)}, u32[]{:S(2)}, u32[]{:S(2)}) %collective-permute-start.1) | collective-permute-done | bytes 524320 | tf_op jit(solution)/shard_map/ppermute | solution.py:245
  30.1 11.2 %collective-permute-done.2.refs_3_ = bf16[128,2048]{1,0:T(8,128)(2,1)S(1)} collective-permute-done((bf16[128,2048]{1,0:T(8,128)(2,1)S(1)}, bf16[128,2048]{1,0:T(8,128)(2,1)S(1)}, u32[]{:S(2)}, u32[]{:S(2)}) %collective-permute-start.2) | collective-permute-done | bytes 524320 | tf_op jit(solution)/shard_map/ppermute | solution.py:245
  41.3 10.3 %shard_map.95 = (bf16[2,256,1536]{2,1,0:T(8,128)(2,1)S(1)}, bf16[2,256,1536]{2,1,0:T(8,128)(2,1)S(1)}) custom-call(s32[8]{0:T(128)S(1)} %dynamic-slice_bitcast_fusion.1.slots, bf16[128,2048]{1,0:T(8,128)(2,1)S(1)} %copy-done, bf16[128,2048]{1,0:T(8,128)(2,1)S(1)} %collective-permute-done.refs_1_, bf16[128,2048]{1,0:T(8,128)(2,1)S(1)} %collective-permute-done.1.refs_2_, ...), custom_call_target="tpu_custom_call" | custom-call | flops 6442450944 | bytes 17825792 | tf_op jit(solution)/shard_map/pallas_call | solution.py:108
  51.6 10.3 %shard_map.96 = (bf16[2,256,1536]{2,1,0:T(8,128)(2,1)S(1)}, bf16[2,256,1536]{2,1,0:T(8,128)(2,1)S(1)}) custom-call(s32[8]{0:T(128)S(1)} %dynamic-slice_bitcast_fusion.1.slots, bf16[128,2048]{1,0:T(8,128)(2,1)S(1)} %copy-done, bf16[128,2048]{1,0:T(8,128)(2,1)S(1)} %collective-permute-done.refs_1_, bf16[128,2048]{1,0:T(8,128)(2,1)S(1)} %collective-permute-done.1.refs_2_, ...), custom_call_target="tpu_custom_call" | custom-call | flops 6442450944 | bytes 17825792 | tf_op jit(solution)/shard_map/pallas_call | solution.py:108
  62.5 10.3 %shard_map.97 = (bf16[2,256,1536]{2,1,0:T(8,128)(2,1)S(1)}, bf16[2,256,1536]{2,1,0:T(8,128)(2,1)S(1)}) custom-call(s32[8]{0:T(128)S(1)} %dynamic-slice_bitcast_fusion.1.slots, bf16[128,2048]{1,0:T(8,128)(2,1)S(1)} %copy-done, bf16[128,2048]{1,0:T(8,128)(2,1)S(1)} %collective-permute-done.refs_1_, bf16[128,2048]{1,0:T(8,128)(2,1)S(1)} %collective-permute-done.1.refs_2_, ...), custom_call_target="tpu_custom_call" | custom-call | flops 6442450944 | bytes 17825792 | tf_op jit(solution)/shard_map/pallas_call | solution.py:108
  72.9 13.4 %shard_map.98 = (bf16[2,256,2048]{2,1,0:T(8,128)(2,1)S(1)}, bf16[2,256,2048]{2,1,0:T(8,128)(2,1)}) custom-call(s32[8]{0:T(128)S(1)} %dynamic-slice_bitcast_fusion.1.slots, bf16[128,2048]{1,0:T(8,128)(2,1)S(1)} %copy-done, bf16[128,2048]{1,0:T(8,128)(2,1)S(1)} %collective-permute-done.refs_1_, bf16[128,2048]{1,0:T(8,128)(2,1)S(1)} %collective-permute-done.1.refs_2_, ...), custom_call_target="tpu_custom_call" | custom-call | flops 8589934592 | bytes 23068672 | tf_op jit(solution)/shard_map/pallas_call | solution.py:108
  96.4 4.6 %collective-permute-done.4 = bf16[2,128,1536]{2,1,0:T(8,128)(2,1)S(1)} collective-permute-done((bf16[2,128,1536]{2,1,0:T(8,128)(2,1)S(1)}, bf16[2,128,1536]{2,1,0:T(8,128)(2,1)S(1)}, u32[]{:S(2)}, u32[]{:S(2)}) %collective-permute-start.4) | collective-permute-done | bytes 786464 | tf_op jit(solution)/shard_map/ppermute | solution.py:48
  103.5 10.1 %collective-permute-done.7 = bf16[2,128,1536]{2,1,0:T(8,128)(2,1)S(1)} collective-permute-done((bf16[2,128,1536]{2,1,0:T(8,128)(2,1)S(1)}, bf16[2,128,1536]{2,1,0:T(8,128)(2,1)S(1)}, u32[]{:S(2)}, u32[]{:S(2)}) %collective-permute-start.7) | collective-permute-done | bytes 786464 | tf_op jit(solution)/shard_map/ppermute | solution.py:48
  116.2 10.1 %collective-permute-done.10 = bf16[2,128,1536]{2,1,0:T(8,128)(2,1)S(1)} collective-permute-done((bf16[2,128,1536]{2,1,0:T(8,128)(2,1)S(1)}, bf16[2,128,1536]{2,1,0:T(8,128)(2,1)S(1)}, u32[]{:S(2)}, u32[]{:S(2)}) %collective-permute-start.10) | collective-permute-done | bytes 786464 | tf_op jit(solution)/shard_map/ppermute | solution.py:48
  131.9 1.6 collective-permute-start.23
  134.0 11.9 %collective-permute-done.13 = bf16[2,128,2048]{2,1,0:T(8,128)(2,1)S(1)} collective-permute-done((bf16[2,128,2048]{2,1,0:T(8,128)(2,1)S(1)}, bf16[2,128,2048]{2,1,0:T(8,128)(2,1)S(1)}, u32[]{:S(2)}, u32[]{:S(2)}) %collective-permute-start.13) | collective-permute-done | bytes 1048608 | tf_op jit(solution)/shard_map/ppermute | solution.py:48
  147.5 2.2 collective-permute-start.14
  151.2 7.9 %collective-permute-done.14 = bf16[2,64,2048]{2,1,0:T(8,128)(2,1)S(1)} collective-permute-done((bf16[2,64,2048]{2,1,0:T(8,128)(2,1)S(1)}, bf16[2,64,2048]{2,1,0:T(8,128)(2,1)S(1)}, u32[]{:S(2)}, u32[]{:S(2)}) %collective-permute-start.14) | collective-permute-done | bytes 524320 | tf_op jit(solution)/shard_map/ppermute | solution.py:48
  164.0 2.8 collective-permute-done.39.refs_1_
  168.1 2.9 %collective-permute-done.24.refs_3_ = bf16[2,32,3072]{2,1,0:T(8,128)(2,1)S(1)} collective-permute-done((bf16[2,32,3072]{2,1,0:T(8,128)(2,1)S(1)}, bf16[2,32,3072]{2,1,0:T(8,128)(2,1)S(1)}, u32[]{:S(2)}, u32[]{:S(2)}) %collective-permute-start.24) | collective-permute-done | bytes 393248 | tf_op jit(solution)/shard_map/ppermute | solution.py:48
  172.8 3.3 %collective-permute-done.41.refs_3_ = bf16[2,32,3072]{2,1,0:T(8,128)(2,1)S(1)} collective-permute-done((bf16[2,32,3072]{2,1,0:T(8,128)(2,1)S(1)}, bf16[2,32,3072]{2,1,0:T(8,128)(2,1)S(1)}, u32[]{:S(2)}, u32[]{:S(2)}) %collective-permute-start.41) | collective-permute-done | bytes 393248 | tf_op jit(solution)/shard_map/ppermute | solution.py:48
  177.7 1.4 collective-permute-start.33
  179.1 1.6 collective-permute-done.16.refs_2_
  182.0 14.1 %shard_map.99.refs_12_ = f32[2048,256]{1,0:T(8,128)S(1)} custom-call(s32[8]{0:T(128)S(1)} %dynamic-slice_bitcast_fusion.where, bf16[2,32,3072]{2,1,0:T(8,128)(2,1)S(1)} %pad_maximum_fusion.3.refs_0_, bf16[2,32,3072]{2,1,0:T(8,128)(2,1)S(1)} %collective-permute-done.22.refs_1_, bf16[2,32,3072]{2,1,0:T(8,128)(2,1)S(1)} %collective-permute-done.23.refs_2_, ...), custom_call_target="tpu_custom_call" | custom-call | flops 6442450944 | bytes 29360128 | tf_op jit(solution)/shard_map/pallas_call | solution.py:196
  196.1 1.4 copy-done.1
  200.0 14.1 %shard_map.101.refs_12_ = f32[2048,256]{1,0:T(8,128)S(1)} custom-call(s32[8]{0:T(128)S(1)} %dynamic-slice_bitcast_fusion.where, bf16[2,32,3072]{2,1,0:T(8,128)(2,1)S(1)} %pad_maximum_fusion.4.refs_0_, bf16[2,32,3072]{2,1,0:T(8,128)(2,1)S(1)} %collective-permute-done.39.refs_1_, bf16[2,32,3072]{2,1,0:T(8,128)(2,1)S(1)} %collective-permute-done.40.refs_2_, ...), custom_call_target="tpu_custom_call" | custom-call | flops 6442450944 | bytes 29360128 | tf_op jit(solution)/shard_map/pallas_call | solution.py:196
  216.6 17.6 %shard_map.100 = (bf16[64,2048]{1,0:T(8,128)(2,1)S(1)}, bf16[64,2048]{1,0:T(8,128)(2,1)S(1)}, bf16[64,2048]{1,0:T(8,128)(2,1)S(1)}, bf16[64,2048]{1,0:T(8,128)(2,1)S(1)}) custom-call(s32[8]{0:T(128)S(1)} %dynamic-slice_bitcast_fusion.where, bf16[2,32,3584]{2,1,0:T(8,128)(2,1)S(1)} %pad_maximum_fusion.1.refs_0_, ...), custom_call_target="tpu_custom_call" | custom-call | flops 7516192768 | bytes 34078720 | tf_op jit(solution)/shard_map/pallas_call | solution.py:196
  234.2 1.8 collective-permute-start.29
  236.3 17.4 %shard_map.102 = (bf16[64,2048]{1,0:T(8,128)(2,1)S(1)}, bf16[64,2048]{1,0:T(8,128)(2,1)S(1)}, bf16[64,2048]{1,0:T(8,128)(2,1)S(1)}, bf16[64,2048]{1,0:T(8,128)(2,1)S(1)}) custom-call(s32[8]{0:T(128)S(1)} %dynamic-slice_bitcast_fusion.where, bf16[2,32,3584]{2,1,0:T(8,128)(2,1)S(1)} %pad_maximum_fusion.2.refs_0_, ...), custom_call_target="tpu_custom_call" | custom-call | flops 7516192768 | bytes 34078720 | tf_op jit(solution)/shard_map/pallas_call | solution.py:196
  253.7 1.8 collective-permute-start.46
  255.9 3.3 %collective-permute-start.30 = (bf16[64,2048]{1,0:T(8,128)(2,1)S(1)}, bf16[64,2048]{1,0:T(8,128)(2,1)S(1)}, u32[]{:S(2)}, u32[]{:S(2)}) collective-permute-start(bf16[64,2048]{1,0:T(8,128)(2,1)S(1)} %add_convert_fusion.11), channel_id=1, source_target_pairs={{0,2},{1,3},{2,0},{3,1},{4,6},{5,7},{6,4},{7,5},{8,10},{9,11},{10,... | collective-permute-start | bytes 786440 | tf_op jit(solution)/shard_map/ppermute | solution.py:245
  259.2 9.4 %collective-permute-done.46 = bf16[64,2048]{1,0:T(8,128)(2,1)S(1)} collective-permute-done((bf16[64,2048]{1,0:T(8,128)(2,1)S(1)}, bf16[64,2048]{1,0:T(8,128)(2,1)S(1)}, u32[]{:S(2)}, u32[]{:S(2)}) %collective-permute-start.46) | collective-permute-done | bytes 262176 | tf_op jit(solution)/shard_map/ppermute | solution.py:245
  268.6 2.6 collective-permute-start.47
  271.3 2.2 collective-permute-done.30
  273.8 12.8 %collective-permute-done.47 = bf16[64,2048]{1,0:T(8,128)(2,1)S(1)} collective-permute-done((bf16[64,2048]{1,0:T(8,128)(2,1)S(1)}, bf16[64,2048]{1,0:T(8,128)(2,1)S(1)}, u32[]{:S(2)}, u32[]{:S(2)}) %collective-permute-start.47) | collective-permute-done | bytes 262176 | tf_op jit(solution)/shard_map/ppermute | solution.py:245
  (124 shorter events, 46.0 us)
Async XLA Ops:
  0.6 27.6 %collective-permute-start.1 = (bf16[128,2048]{1,0:T(8,128)(2,1)}, bf16[128,2048]{1,0:T(8,128)(2,1)S(1)}, u32[]{:S(2)}, u32[]{:S(2)}) collective-permute-start(bf16[128,2048]{1,0:T(8,128)(2,1)} %refs_0_.7), channel_id=1, source_target_pairs={{0,2},{1,3},{2,0},{3,1},{4,6},{5,7},{6,4},{7,5},{8,10},{9,11},{10,... | collective-permute-start | bytes 1572872 | tf_op jit(solution)/shard_map/ppermute | solution.py:245
  4.7 25.3 %collective-permute-start = (bf16[128,2048]{1,0:T(8,128)(2,1)}, bf16[128,2048]{1,0:T(8,128)(2,1)S(1)}, u32[]{:S(2)}, u32[]{:S(2)}) collective-permute-start(bf16[128,2048]{1,0:T(8,128)(2,1)} %refs_0_.7), channel_id=1, source_target_pairs={{0,1},{1,0},{2,3},{3,2},{4,5},{5,4},{6,7},{7,6},{8,9},{9,8},{10,11... | collective-permute-start | bytes 1572872 | tf_op jit(solution)/shard_map/ppermute | solution.py:245
  51.6 36.0 %collective-permute-start.3 = (bf16[2,256,1536]{2,1,0:T(8,128)(2,1)S(1)}, bf16[2,256,1536]{2,1,0:T(8,128)(2,1)}, u32[]{:S(2)}, u32[]{:S(2)}) collective-permute-start(bf16[2,256,1536]{2,1,0:T(8,128)(2,1)S(1)} %get-tuple-element.19), channel_id=1, source_target_pairs={{0,4},{4,0},{8,12},{12,8},{16,20},{20,16},{24,28},{28,24},{1,5},{5... | collective-permute-start | bytes 4718600 | tf_op jit(solution)/shard_map/ppermute | solution.py:51
  62.0 28.3 %collective-permute-start.6 = (bf16[2,256,1536]{2,1,0:T(8,128)(2,1)S(1)}, bf16[2,256,1536]{2,1,0:T(8,128)(2,1)}, u32[]{:S(2)}, u32[]{:S(2)}) collective-permute-start(bf16[2,256,1536]{2,1,0:T(8,128)(2,1)S(1)} %get-tuple-element.21), channel_id=1, source_target_pairs={{0,4},{4,0},{8,12},{12,8},{16,20},{20,16},{24,28},{28,24},{1,5},{5... | collective-permute-start | bytes 4718600 | tf_op jit(solution)/shard_map/ppermute | solution.py:51
  72.8 19.6 %collective-permute-start.9 = (bf16[2,256,1536]{2,1,0:T(8,128)(2,1)S(1)}, bf16[2,256,1536]{2,1,0:T(8,128)(2,1)}, u32[]{:S(2)}, u32[]{:S(2)}) collective-permute-start(bf16[2,256,1536]{2,1,0:T(8,128)(2,1)S(1)} %get-tuple-element.23), channel_id=1, source_target_pairs={{0,4},{4,0},{8,12},{12,8},{16,20},{20,16},{24,28},{28,24},{1,5},{5... | collective-permute-start | bytes 4718600 | tf_op jit(solution)/shard_map/ppermute | solution.py:51
  91.6 22.0 %collective-permute-start.7 = (bf16[2,128,1536]{2,1,0:T(8,128)(2,1)S(1)}, bf16[2,128,1536]{2,1,0:T(8,128)(2,1)S(1)}, u32[]{:S(2)}, u32[]{:S(2)}) collective-permute-start(bf16[2,128,1536]{2,1,0:T(8,128)(2,1)S(1)} %add_convert_fusion.2), channel_id=1, source_target_pairs={{0,8},{4,20},{8,0},{12,28},{16,24},{20,4},{24,16},{28,12},{1,9},{5... | collective-permute-start | bytes 2359304 | tf_op jit(solution)/shard_map/ppermute | solution.py:48
  93.8 32.4 %collective-permute-start.10 = (bf16[2,128,1536]{2,1,0:T(8,128)(2,1)S(1)}, bf16[2,128,1536]{2,1,0:T(8,128)(2,1)S(1)}, u32[]{:S(2)}, u32[]{:S(2)}) collective-permute-start(bf16[2,128,1536]{2,1,0:T(8,128)(2,1)S(1)} %add_convert_fusion.1), channel_id=1, source_target_pairs={{0,8},{4,20},{8,0},{12,28},{16,24},{20,4},{24,16},{28,12},{1,9},{5... | collective-permute-start | bytes 2359304 | tf_op jit(solution)/shard_map/ppermute | solution.py:48
  95.6 50.4 %collective-permute-start.13 = (bf16[2,128,2048]{2,1,0:T(8,128)(2,1)S(1)}, bf16[2,128,2048]{2,1,0:T(8,128)(2,1)S(1)}, u32[]{:S(2)}, u32[]{:S(2)}) collective-permute-start(bf16[2,128,2048]{2,1,0:T(8,128)(2,1)S(1)} %add_convert_fusion), channel_id=1, source_target_pairs={{0,8},{4,20},{8,0},{12,28},{16,24},{20,4},{24,16},{28,12},{1,9},{5... | collective-permute-start | bytes 3145736 | tf_op jit(solution)/shard_map/ppermute | solution.py:48
  102.2 26.6 %collective-permute-start.5 = (bf16[2,64,1536]{2,1,0:T(8,128)(2,1)S(1)}, bf16[2,64,1536]{2,1,0:T(8,128)(2,1)S(1)}, u32[]{:S(2)}, u32[]{:S(2)}) collective-permute-start(bf16[2,64,1536]{2,1,0:T(8,128)(2,1)S(1)} %add_convert_fusion.7), channel_id=1, source_target_pairs={{0,16},{4,12},{8,24},{12,4},{16,0},{20,28},{24,8},{28,20},{1,17},{... | collective-permute-start | bytes 1179656 | tf_op jit(solution)/shard_map/ppermute | solution.py:48
  127.5 20.0 %collective-permute-start.11 = (bf16[2,64,1536]{2,1,0:T(8,128)(2,1)S(1)}, bf16[2,64,1536]{2,1,0:T(8,128)(2,1)S(1)}, u32[]{:S(2)}, u32[]{:S(2)}) collective-permute-start(bf16[2,64,1536]{2,1,0:T(8,128)(2,1)S(1)} %add_convert_fusion.5), channel_id=1, source_target_pairs={{0,16},{4,12},{8,24},{12,4},{16,0},{20,28},{24,8},{28,20},{1,17},{... | collective-permute-start | bytes 1179656 | tf_op jit(solution)/shard_map/ppermute | solution.py:48
  131.9 30.2 %collective-permute-start.23 = (bf16[2,32,3072]{2,1,0:T(8,128)(2,1)S(1)}, bf16[2,32,3072]{2,1,0:T(8,128)(2,1)S(1)}, u32[]{:S(2)}, u32[]{:S(2)}) collective-permute-start(bf16[2,32,3072]{2,1,0:T(8,128)(2,1)S(1)} %pad_maximum_fusion.3.refs_0_), channel_id=1, source_target_pairs={{0,8},{4,20},{8,0},{12,28},{16,24},{20,4},{24,16},{28,12},{1,9},{5... | collective-permute-start | bytes 1179656 | tf_op jit(solution)/shard_map/ppermute | solution.py:48
  133.4 28.7 %collective-permute-start.22 = (bf16[2,32,3072]{2,1,0:T(8,128)(2,1)S(1)}, bf16[2,32,3072]{2,1,0:T(8,128)(2,1)S(1)}, u32[]{:S(2)}, u32[]{:S(2)}) collective-permute-start(bf16[2,32,3072]{2,1,0:T(8,128)(2,1)S(1)} %pad_maximum_fusion.3.refs_0_), channel_id=1, source_target_pairs={{0,16},{4,12},{8,24},{12,4},{16,0},{20,28},{24,8},{28,20},{1,17},{... | collective-permute-start | bytes 1179656 | tf_op jit(solution)/shard_map/ppermute | solution.py:48
  133.9 29.0 %collective-permute-start.25 = (bf16[2,32,3072]{2,1,0:T(8,128)(2,1)S(1)}, bf16[2,32,3072]{2,1,0:T(8,128)(2,1)S(1)}, u32[]{:S(2)}, u32[]{:S(2)}) collective-permute-start(bf16[2,32,3072]{2,1,0:T(8,128)(2,1)S(1)} %pad_maximum_fusion.3.refs_0_), channel_id=1, source_target_pairs={{0,4},{4,0},{8,12},{12,8},{16,20},{20,16},{24,28},{28,24},{1,5},{5... | collective-permute-start | bytes 1179656 | tf_op jit(solution)/shard_map/ppermute | solution.py:51
  145.9 17.9 %collective-permute-start.40 = (bf16[2,32,3072]{2,1,0:T(8,128)(2,1)S(1)}, bf16[2,32,3072]{2,1,0:T(8,128)(2,1)S(1)}, u32[]{:S(2)}, u32[]{:S(2)}) collective-permute-start(bf16[2,32,3072]{2,1,0:T(8,128)(2,1)S(1)} %pad_maximum_fusion.4.refs_0_), channel_id=1, source_target_pairs={{0,8},{4,20},{8,0},{12,28},{16,24},{20,4},{24,16},{28,12},{1,9},{5... | collective-permute-start | bytes 1179656 | tf_op jit(solution)/shard_map/ppermute | solution.py:48
  176.2 21.2 %collective-permute-start.45 = (bf16[2,32,3072]{2,1,0:T(8,128)(2,1)S(1)}, bf16[2,32,3072]{2,1,0:T(8,128)(2,1)S(1)}, u32[]{:S(2)}, u32[]{:S(2)}) collective-permute-start(bf16[2,32,3072]{2,1,0:T(8,128)(2,1)S(1)} %collective-permute-done.41.refs_3_), channel_id=1, source_target_pairs={{0,4},{4,0},{8,12},{12,8},{16,20},{20,16},{24,28},{28,24},{1,5},{5... | collective-permute-start | bytes 1179656 | tf_op jit(solution)/shard_map/ppermute | solution.py:51
  176.2 22.0 %collective-permute-start.15 = (bf16[2,32,3584]{2,1,0:T(8,128)(2,1)S(1)}, bf16[2,32,3584]{2,1,0:T(8,128)(2,1)S(1)}, u32[]{:S(2)}, u32[]{:S(2)}) collective-permute-start(bf16[2,32,3584]{2,1,0:T(8,128)(2,1)S(1)} %pad_maximum_fusion.1.refs_0_), channel_id=1, source_target_pairs={{0,16},{4,12},{8,24},{12,4},{16,0},{20,28},{24,8},{28,20},{1,17},{... | collective-permute-start | bytes 1376264 | tf_op jit(solution)/shard_map/ppermute | solution.py:48
  177.5 20.7 %collective-permute-start.18 = (bf16[2,32,3584]{2,1,0:T(8,128)(2,1)S(1)}, bf16[2,32,3584]{2,1,0:T(8,128)(2,1)S(1)}, u32[]{:S(2)}, u32[]{:S(2)}) collective-permute-start(bf16[2,32,3584]{2,1,0:T(8,128)(2,1)S(1)} %pad_maximum_fusion.1.refs_0_), channel_id=1, source_target_pairs={{0,4},{4,0},{8,12},{12,8},{16,20},{20,16},{24,28},{28,24},{1,5},{5... | collective-permute-start | bytes 1376264 | tf_op jit(solution)/shard_map/ppermute | solution.py:51
  177.7 21.0 %collective-permute-start.33 = (bf16[2,32,3584]{2,1,0:T(8,128)(2,1)S(1)}, bf16[2,32,3584]{2,1,0:T(8,128)(2,1)S(1)}, u32[]{:S(2)}, u32[]{:S(2)}) collective-permute-start(bf16[2,32,3584]{2,1,0:T(8,128)(2,1)S(1)} %pad_maximum_fusion.2.refs_0_), channel_id=1, source_target_pairs={{0,8},{4,20},{8,0},{12,28},{16,24},{20,4},{24,16},{28,12},{1,9},{5... | collective-permute-start | bytes 1376264 | tf_op jit(solution)/shard_map/ppermute | solution.py:48
  180.7 19.3 %collective-permute-start.17 = (bf16[2,32,3584]{2,1,0:T(8,128)(2,1)S(1)}, bf16[2,32,3584]{2,1,0:T(8,128)(2,1)S(1)}, u32[]{:S(2)}, u32[]{:S(2)}) collective-permute-start(bf16[2,32,3584]{2,1,0:T(8,128)(2,1)S(1)} %collective-permute-done.16.refs_2_), channel_id=1, source_target_pairs={{0,16},{4,12},{8,24},{12,4},{16,0},{20,28},{24,8},{28,20},{1,17},{... | collective-permute-start | bytes 1376264 | tf_op jit(solution)/shard_map/ppermute | solution.py:48
  197.4 18.0 %collective-permute-start.32 = (bf16[2,32,3584]{2,1,0:T(8,128)(2,1)S(1)}, bf16[2,32,3584]{2,1,0:T(8,128)(2,1)S(1)}, u32[]{:S(2)}, u32[]{:S(2)}) collective-permute-start(bf16[2,32,3584]{2,1,0:T(8,128)(2,1)S(1)} %pad_maximum_fusion.2.refs_0_), channel_id=1, source_target_pairs={{0,16},{4,12},{8,24},{12,4},{16,0},{20,28},{24,8},{28,20},{1,17},{... | collective-permute-start | bytes 1376264 | tf_op jit(solution)/shard_map/ppermute | solution.py:48
  198.2 17.9 %collective-permute-start.20 = (bf16[2,32,3584]{2,1,0:T(8,128)(2,1)S(1)}, bf16[2,32,3584]{2,1,0:T(8,128)(2,1)S(1)}, u32[]{:S(2)}, u32[]{:S(2)}) collective-permute-start(bf16[2,32,3584]{2,1,0:T(8,128)(2,1)S(1)} %collective-permute-done.16.refs_2_), channel_id=1, source_target_pairs={{0,4},{4,0},{8,12},{12,8},{16,20},{20,16},{24,28},{28,24},{1,5},{5... | collective-permute-start | bytes 1376264 | tf_op jit(solution)/shard_map/ppermute | solution.py:51
  198.2 17.8 %collective-permute-start.19 = (bf16[2,32,3584]{2,1,0:T(8,128)(2,1)S(1)}, bf16[2,32,3584]{2,1,0:T(8,128)(2,1)S(1)}, u32[]{:S(2)}, u32[]{:S(2)}) collective-permute-start(bf16[2,32,3584]{2,1,0:T(8,128)(2,1)S(1)} %collective-permute-done.15.refs_1_), channel_id=1, source_target_pairs={{0,4},{4,0},{8,12},{12,8},{16,20},{20,16},{24,28},{28,24},{1,5},{5... | collective-permute-start | bytes 1376264 | tf_op jit(solution)/shard_map/ppermute | solution.py:51
  198.7 17.8 %collective-permute-start.34 = (bf16[2,32,3584]{2,1,0:T(8,128)(2,1)S(1)}, bf16[2,32,3584]{2,1,0:T(8,128)(2,1)S(1)}, u32[]{:S(2)}, u32[]{:S(2)}) collective-permute-start(bf16[2,32,3584]{2,1,0:T(8,128)(2,1)S(1)} %collective-permute-done.33.refs_2_), channel_id=1, source_target_pairs={{0,16},{4,12},{8,24},{12,4},{16,0},{20,28},{24,8},{28,20},{1,17},{... | collective-permute-start | bytes 1376264 | tf_op jit(solution)/shard_map/ppermute | solution.py:48
  215.5 20.5 %collective-permute-start.35 = (bf16[2,32,3584]{2,1,0:T(8,128)(2,1)S(1)}, bf16[2,32,3584]{2,1,0:T(8,128)(2,1)S(1)}, u32[]{:S(2)}, u32[]{:S(2)}) collective-permute-start(bf16[2,32,3584]{2,1,0:T(8,128)(2,1)S(1)} %pad_maximum_fusion.2.refs_0_), channel_id=1, source_target_pairs={{0,4},{4,0},{8,12},{12,8},{16,20},{20,16},{24,28},{28,24},{1,5},{5... | collective-permute-start | bytes 1376264 | tf_op jit(solution)/shard_map/ppermute | solution.py:51
  216.0 20.3 %collective-permute-start.37 = (bf16[2,32,3584]{2,1,0:T(8,128)(2,1)S(1)}, bf16[2,32,3584]{2,1,0:T(8,128)(2,1)S(1)}, u32[]{:S(2)}, u32[]{:S(2)}) collective-permute-start(bf16[2,32,3584]{2,1,0:T(8,128)(2,1)S(1)} %collective-permute-done.33.refs_2_), channel_id=1, source_target_pairs={{0,4},{4,0},{8,12},{12,8},{16,20},{20,16},{24,28},{28,24},{1,5},{5... | collective-permute-start | bytes 1376264 | tf_op jit(solution)/shard_map/ppermute | solution.py:51
  216.1 20.2 %collective-permute-start.36 = (bf16[2,32,3584]{2,1,0:T(8,128)(2,1)S(1)}, bf16[2,32,3584]{2,1,0:T(8,128)(2,1)S(1)}, u32[]{:S(2)}, u32[]{:S(2)}) collective-permute-start(bf16[2,32,3584]{2,1,0:T(8,128)(2,1)S(1)} %collective-permute-done.32.refs_1_), channel_id=1, source_target_pairs={{0,4},{4,0},{8,12},{12,8},{16,20},{20,16},{24,28},{28,24},{1,5},{5... | collective-permute-start | bytes 1376264 | tf_op jit(solution)/shard_map/ppermute | solution.py:51
  216.5 19.8 %collective-permute-start.38 = (bf16[2,32,3584]{2,1,0:T(8,128)(2,1)S(1)}, bf16[2,32,3584]{2,1,0:T(8,128)(2,1)S(1)}, u32[]{:S(2)}, u32[]{:S(2)}) collective-permute-start(bf16[2,32,3584]{2,1,0:T(8,128)(2,1)S(1)} %collective-permute-done.34.refs_3_), channel_id=1, source_target_pairs={{0,4},{4,0},{8,12},{12,8},{16,20},{20,16},{24,28},{28,24},{1,5},{5... | collective-permute-start | bytes 1376264 | tf_op jit(solution)/shard_map/ppermute | solution.py:51
  234.2 21.6 %collective-permute-start.29 = (bf16[64,2048]{1,0:T(8,128)(2,1)S(1)}, bf16[64,2048]{1,0:T(8,128)(2,1)S(1)}, u32[]{:S(2)}, u32[]{:S(2)}) collective-permute-start(bf16[64,2048]{1,0:T(8,128)(2,1)S(1)} %get-tuple-element.28), channel_id=1, source_target_pairs={{0,1},{1,0},{2,3},{3,2},{4,5},{5,4},{6,7},{7,6},{8,9},{9,8},{10,11... | collective-permute-start | bytes 786440 | tf_op jit(solution)/shard_map/ppermute | solution.py:245
  236.0 35.3 %collective-permute-start.31 = (bf16[64,2048]{1,0:T(8,128)(2,1)S(1)}, bf16[64,2048]{1,0:T(8,128)(2,1)S(1)}, u32[]{:S(2)}, u32[]{:S(2)}) collective-permute-start(bf16[64,2048]{1,0:T(8,128)(2,1)S(1)} %get-tuple-element.29), channel_id=1, source_target_pairs={{0,1},{1,0},{2,3},{3,2},{4,5},{5,4},{6,7},{7,6},{8,9},{9,8},{10,11... | collective-permute-start | bytes 786440 | tf_op jit(solution)/shard_map/ppermute | solution.py:245
  255.5 18.3 %collective-permute-start.48 = (bf16[64,2048]{1,0:T(8,128)(2,1)S(1)}, bf16[64,2048]{1,0:T(8,128)(2,1)S(1)}, u32[]{:S(2)}, u32[]{:S(2)}) collective-permute-start(bf16[64,2048]{1,0:T(8,128)(2,1)S(1)} %get-tuple-element.33), channel_id=1, source_target_pairs={{0,1},{1,0},{2,3},{3,2},{4,5},{5,4},{6,7},{7,6},{8,9},{9,8},{10,11... | collective-permute-start | bytes 786440 | tf_op jit(solution)/shard_map/ppermute | solution.py:245
  255.9 17.6 %collective-permute-start.30 = (bf16[64,2048]{1,0:T(8,128)(2,1)S(1)}, bf16[64,2048]{1,0:T(8,128)(2,1)S(1)}, u32[]{:S(2)}, u32[]{:S(2)}) collective-permute-start(bf16[64,2048]{1,0:T(8,128)(2,1)S(1)} %add_convert_fusion.11), channel_id=1, source_target_pairs={{0,2},{1,3},{2,0},{3,1},{4,6},{5,7},{6,4},{7,5},{8,10},{9,11},{10,... | collective-permute-start | bytes 786440 | tf_op jit(solution)/shard_map/ppermute | solution.py:245
  268.6 18.0 %collective-permute-start.47 = (bf16[64,2048]{1,0:T(8,128)(2,1)S(1)}, bf16[64,2048]{1,0:T(8,128)(2,1)S(1)}, u32[]{:S(2)}, u32[]{:S(2)}) collective-permute-start(bf16[64,2048]{1,0:T(8,128)(2,1)S(1)} %add_convert_fusion.9), channel_id=1, source_target_pairs={{0,2},{1,3},{2,0},{3,1},{4,6},{5,7},{6,4},{7,5},{8,10},{9,11},{10,... | collective-permute-start | bytes 786440 | tf_op jit(solution)/shard_map/ppermute | solution.py:245
  (21 other events, 229.2 us)
